TPU v7x, 256 devices: a whole 4x4x8 slice. The times are simulated.
256 devices in a mesh: row: 16 (over y, z_lo, core), col: 16 (over z_hi, x).
Axes of the slice: x: 4, y: 4, z: 8 (z_hi: 4, z_lo: 2; z = z_hi * 2 + z_lo), core: 2. Of those that a mesh axis runs over, the one named last changes fastest.
Arguments:
- node_feats: bfloat16 [65536, 256], P(('col', 'row')), may hold values from -6 to 6
- weight: bfloat16 [256, 256], replicated, may hold values from -0.375 to 0.375
- bias: float32 [256], replicated, may hold values from -3 to 3
- cotangent: bfloat16 [65536, 256], P(('row', 'col')), may hold values from -6 to 6
- tiles: bfloat16 [16, 16, 192, 128, 128], P('row', 'col'), as said below
- coords: int32 [16, 16, 192, 2], P('row', 'col'), may hold values from 0 to 31, as said below
- counts: int32 [16, 16], P('row', 'col'), may hold values from 24 to 192, as said below
Outputs:
- activations: bfloat16 [65536, 256], P(('row', 'col'))
- weight_grad: float32 [256, 256], replicated
- bias_grad: float32 [256], replicated
- feats_grad: bfloat16 [65536, 256], P(('col', 'row'))
Inputs may be any that keep to these rules, and one draw needn't show every extreme that they name: `coords`: within one block the 192 slots name distinct tile positions; the row is below 32 and the column below 32, also in slots that are not live; every block holds the position (31, 31) in some slot. Live slot counts of the blocks vary widely; some block has all 192 slots live. `tiles`: entries are zero or positive.
All inputs are finite; a program needn't handle non-finite values.
Results may differ from a plain program's by a relative error of at most 0.008.
Values may be sent and summed in bfloat16 or wider, within the bound.
A program may use at most 128 MiB of HBM per device.

v0:
```python
import jax
import jax.numpy as jnp
from jax import lax
from jax.sharding import PartitionSpec as P


def tile_products(values, places, live_count, offset, source, rows_out, transposed):
    slots = values.shape[0]
    side = values.shape[1]
    feats = source.shape[1]
    src_tiles = source.reshape(-1, side, feats)
    width = min(32, slots)
    read_at = 0 if transposed else 1
    write_at = 1 if transposed else 0
    form = "bji,bjf->bif" if transposed else "bij,bjf->bif"

    def step(block, acc):
        start = block * width
        piece = lax.dynamic_slice_in_dim(values, start, width, 0)
        where_at = lax.dynamic_slice_in_dim(places, start, width, 0)
        live = offset + start + jnp.arange(width, dtype=jnp.int32) < live_count
        taken = src_tiles[where_at[:, read_at]]
        product = jnp.einsum(form, piece, taken, preferred_element_type=jnp.float32)
        product = jnp.where(live[:, None, None], product, 0.0)
        return acc.at[where_at[:, write_at]].add(product)

    acc = jnp.zeros((rows_out // side, side, feats), jnp.float32)
    upper = slots // width
    acc = lax.fori_loop(0, upper, step, acc)
    return acc.reshape(rows_out, feats)


def local_grads(pre, cotangent, weight):
    gate = jax.nn.sigmoid(pre)
    activations = (pre * gate).astype(jnp.bfloat16)
    pre_grad = (cotangent.astype(jnp.float32) * gate * (1.0 + pre * (1.0 - gate))).astype(
        jnp.bfloat16
    )
    agg_grad = jnp.dot(pre_grad, weight.T, preferred_element_type=jnp.float32).astype(jnp.bfloat16)
    return (activations, pre_grad, agg_grad)


def body(node_feats, weight, bias, cotangent, tiles, coords, counts):
    nodes_here = node_feats.shape[0]
    row_span = nodes_here * lax.axis_size("col")
    col_span = nodes_here * lax.axis_size("row")
    own_values = tiles[0, 0]
    own_places = coords[0, 0]
    own_count = counts[0, 0]
    column_feats = lax.all_gather(node_feats, "row", axis=0, tiled=True)
    partial_value = tile_products(
        own_values, own_places, own_count, 0, column_feats, row_span, False
    )
    aggregated = lax.psum_scatter(partial_value, "col", scatter_dimension=0, tiled=True).astype(
        jnp.bfloat16
    )
    pre = jnp.dot(aggregated, weight, preferred_element_type=jnp.float32) + bias
    activations, pre_grad, agg_grad = local_grads(pre, cotangent, weight)
    row_grad = lax.all_gather(agg_grad, "col", axis=0, tiled=True)
    weight_part = jnp.dot(aggregated.T, pre_grad, preferred_element_type=jnp.float32)
    bias_part = jnp.sum(pre_grad.astype(jnp.float32), axis=0)
    back_partial = tile_products(own_values, own_places, own_count, 0, row_grad, col_span, True)
    weight_grad, bias_grad = lax.psum((weight_part, bias_part), ("row", "col"))
    feats_grad = lax.psum_scatter(back_partial, "row", scatter_dimension=0, tiled=True).astype(
        jnp.bfloat16
    )
    return (activations, weight_grad, bias_grad, feats_grad)


def solution(mesh):
    return jax.shard_map(
        body,
        mesh=mesh,
        in_specs=(
            P(("col", "row"), None),
            P(),
            P(),
            P(("row", "col"), None),
            P("row", "col", None, None, None),
            P("row", "col", None, None),
            P("row", "col"),
        ),
        out_specs=(P(("row", "col"), None), P(), P(), P(("col", "row"), None)),
        check_vma=False,
    )
```

profile of v0, /device:TPU:1, one launch (start us, length us, event | category | flops | bytes accessed | tf_op | source)
XLA Modules:
  0.0 747.0 jit_solution(6627412503908360124)
XLA Ops:
  8.0 42.7 %all-gather.3.cloned.1.call-done = bf16[4096,256]{1,0:T(8,128)(2,1)} async-done(((bf16[256,256]{1,0:T(8,128)(2,1)}), bf16[4096,256]{1,0:T(8,128)(2,1)}) %all-gather.3.cloned.1.call-update) | async-done | bytes 2097168 | tf_op jit(solution)/shard_map/all_gather | solution.py:50
  53.1 101.0 %while.26 = (s32[]{:T(128)}, f32[32,128,256]{2,1,0:T(8,128)}, s32[192,2]{0,1:T(2,128)S(1)}, s32[]{:T(128)}, bf16[192,128,128]{2,1,0:T(8,128)(2,1)}, /*index=5*/b...) while((s32[]{:T(128)}, f32[32,128,256]{2,1,0:T(8,128)}, s32[192,2]{0,1:T(2,128)S(1)}, ...), condition=%wide.region_2.3_spmd, body=%wide.region_0.2_spmd.sunk | while | flops 270533888 | bytes 24122980 | solution.py:29
  60.0 10.0 %scatter_fusion = f32[32,128,256]{2,1,0:T(8,128)} fusion(f32[32,128,256]{2,1,0:T(8,128)} %get-tuple-element.354, s32[32]{0:T(128)S(1)} %get-tuple-element.333, f32[32,128,256]{2,1,0:T(8,128)} %convolution_select_fusion.4), kind=kCustom, calls=%fused_computation.2.clone.1 | custom fusion | flops 1048576 | bytes 12583040 | tf_op jit(solution)/shard_map/while/body/eval_jaxpr/scatter-add | solution.py:25
  76.9 10.0 %scatter_fusion = f32[32,128,256]{2,1,0:T(8,128)} fusion(f32[32,128,256]{2,1,0:T(8,128)} %get-tuple-element.354, s32[32]{0:T(128)S(1)} %get-tuple-element.333, f32[32,128,256]{2,1,0:T(8,128)} %convolution_select_fusion.4), kind=kCustom, calls=%fused_computation.2.clone.1 | custom fusion | flops 1048576 | bytes 12583040 | tf_op jit(solution)/shard_map/while/body/eval_jaxpr/scatter-add | solution.py:25
  93.8 10.0 %scatter_fusion = f32[32,128,256]{2,1,0:T(8,128)} fusion(f32[32,128,256]{2,1,0:T(8,128)} %get-tuple-element.354, s32[32]{0:T(128)S(1)} %get-tuple-element.333, f32[32,128,256]{2,1,0:T(8,128)} %convolution_select_fusion.4), kind=kCustom, calls=%fused_computation.2.clone.1 | custom fusion | flops 1048576 | bytes 12583040 | tf_op jit(solution)/shard_map/while/body/eval_jaxpr/scatter-add | solution.py:25
  110.6 9.9 %scatter_fusion = f32[32,128,256]{2,1,0:T(8,128)} fusion(f32[32,128,256]{2,1,0:T(8,128)} %get-tuple-element.354, s32[32]{0:T(128)S(1)} %get-tuple-element.333, f32[32,128,256]{2,1,0:T(8,128)} %convolution_select_fusion.4), kind=kCustom, calls=%fused_computation.2.clone.1 | custom fusion | flops 1048576 | bytes 12583040 | tf_op jit(solution)/shard_map/while/body/eval_jaxpr/scatter-add | solution.py:25
  127.4 9.9 %scatter_fusion = f32[32,128,256]{2,1,0:T(8,128)} fusion(f32[32,128,256]{2,1,0:T(8,128)} %get-tuple-element.354, s32[32]{0:T(128)S(1)} %get-tuple-element.333, f32[32,128,256]{2,1,0:T(8,128)} %convolution_select_fusion.4), kind=kCustom, calls=%fused_computation.2.clone.1 | custom fusion | flops 1048576 | bytes 12583040 | tf_op jit(solution)/shard_map/while/body/eval_jaxpr/scatter-add | solution.py:25
  144.2 10.0 %scatter_fusion = f32[32,128,256]{2,1,0:T(8,128)} fusion(f32[32,128,256]{2,1,0:T(8,128)} %get-tuple-element.354, s32[32]{0:T(128)S(1)} %get-tuple-element.333, f32[32,128,256]{2,1,0:T(8,128)} %convolution_select_fusion.4), kind=kCustom, calls=%fused_computation.2.clone.1 | custom fusion | flops 1048576 | bytes 12583040 | tf_op jit(solution)/shard_map/while/body/eval_jaxpr/scatter-add | solution.py:25
  154.2 94.4 %reduce-scatter.3.cloned.1.call-done = f32[256,256]{1,0:T(8,128)} async-done(((f32[4096,256]{1,0:T(8,128)}), f32[256,256]{1,0:T(8,128)}) %reduce-scatter.3.cloned.1.call-update) | async-done | bytes 262160 | tf_op jit(solution)/shard_map/reduce_scatter | solution.py:54
  251.5 8.6 %copy.11 = bf16[1,1,192,128,128]{3,4,2,1,0:T(8,128)(2,1)} copy(bf16[1,1,192,128,128]{4,3,2,1,0:T(8,128)(2,1)} %bitcast.35) | data formatting | bytes 12582912 | tf_op args[4]
  260.1 49.4 %all-gather.5.cloned.1.call-done = bf16[4096,256]{1,0:T(8,128)(2,1)} async-done(((bf16[256,256]{1,0:T(8,128)(2,1)}), bf16[4096,256]{1,0:T(8,128)(2,1)}) %all-gather.5.cloned.1.call-update) | async-done | bytes 2097168 | tf_op jit(solution)/shard_map/all_gather | solution.py:59
  312.1 101.2 %while.27 = (s32[]{:T(128)}, f32[32,128,256]{2,1,0:T(8,128)}, s32[192,2]{0,1:T(2,128)S(1)}, s32[]{:T(128)}, bf16[192,128,128]{1,2,0:T(8,128)(2,1)}, /*index=5*/b...) while((s32[]{:T(128)}, f32[32,128,256]{2,1,0:T(8,128)}, s32[192,2]{0,1:T(2,128)S(1)}, ...), condition=%wide.region_9.10_spmd, body=%wide.region_7.0_spmd.sunk | while | flops 270533888 | bytes 24122980 | solution.py:29
  315.1 3.9 convolution_select_fusion.5
  319.1 9.9 %scatter_fusion.1 = f32[32,128,256]{2,1,0:T(8,128)} fusion(f32[32,128,256]{2,1,0:T(8,128)} %get-tuple-element.384, s32[32]{0:T(128)S(1)} %get-tuple-element.341, f32[32,128,256]{2,1,0:T(8,128)} %convolution_select_fusion.5), kind=kCustom, calls=%fused_computation.3.clone.1 | custom fusion | flops 1048576 | bytes 12583040 | tf_op jit(solution)/shard_map/while/body/eval_jaxpr/scatter-add | solution.py:25
  336.0 9.9 %scatter_fusion.1 = f32[32,128,256]{2,1,0:T(8,128)} fusion(f32[32,128,256]{2,1,0:T(8,128)} %get-tuple-element.384, s32[32]{0:T(128)S(1)} %get-tuple-element.341, f32[32,128,256]{2,1,0:T(8,128)} %convolution_select_fusion.5), kind=kCustom, calls=%fused_computation.3.clone.1 | custom fusion | flops 1048576 | bytes 12583040 | tf_op jit(solution)/shard_map/while/body/eval_jaxpr/scatter-add | solution.py:25
  348.9 3.9 convolution_select_fusion.5
  352.8 10.0 %scatter_fusion.1 = f32[32,128,256]{2,1,0:T(8,128)} fusion(f32[32,128,256]{2,1,0:T(8,128)} %get-tuple-element.384, s32[32]{0:T(128)S(1)} %get-tuple-element.341, f32[32,128,256]{2,1,0:T(8,128)} %convolution_select_fusion.5), kind=kCustom, calls=%fused_computation.3.clone.1 | custom fusion | flops 1048576 | bytes 12583040 | tf_op jit(solution)/shard_map/while/body/eval_jaxpr/scatter-add | solution.py:25
  369.7 9.8 %scatter_fusion.1 = f32[32,128,256]{2,1,0:T(8,128)} fusion(f32[32,128,256]{2,1,0:T(8,128)} %get-tuple-element.384, s32[32]{0:T(128)S(1)} %get-tuple-element.341, f32[32,128,256]{2,1,0:T(8,128)} %convolution_select_fusion.5), kind=kCustom, calls=%fused_computation.3.clone.1 | custom fusion | flops 1048576 | bytes 12583040 | tf_op jit(solution)/shard_map/while/body/eval_jaxpr/scatter-add | solution.py:25
  382.6 3.9 convolution_select_fusion.5
  386.5 10.0 %scatter_fusion.1 = f32[32,128,256]{2,1,0:T(8,128)} fusion(f32[32,128,256]{2,1,0:T(8,128)} %get-tuple-element.384, s32[32]{0:T(128)S(1)} %get-tuple-element.341, f32[32,128,256]{2,1,0:T(8,128)} %convolution_select_fusion.5), kind=kCustom, calls=%fused_computation.3.clone.1 | custom fusion | flops 1048576 | bytes 12583040 | tf_op jit(solution)/shard_map/while/body/eval_jaxpr/scatter-add | solution.py:25
  399.6 3.9 convolution_select_fusion.5
  403.5 9.8 %scatter_fusion.1 = f32[32,128,256]{2,1,0:T(8,128)} fusion(f32[32,128,256]{2,1,0:T(8,128)} %get-tuple-element.384, s32[32]{0:T(128)S(1)} %get-tuple-element.341, f32[32,128,256]{2,1,0:T(8,128)} %convolution_select_fusion.5), kind=kCustom, calls=%fused_computation.3.clone.1 | custom fusion | flops 1048576 | bytes 12583040 | tf_op jit(solution)/shard_map/while/body/eval_jaxpr/scatter-add | solution.py:25
  415.2 76.8 %psum.15 = f32[256]{0:T(256)} all-reduce(f32[256]{0:T(256)S(1)} %get-tuple-element.254), channel_id=1, replica_groups=mesh['row'=16,'col'=16] {'row','col'}, use_global_device_ids=true, to_apply=%region_6.0 | all-reduce | flops 256 | bytes 2048 | tf_op jit(solution)/shard_map/psum | solution.py:63
  493.6 245.2 %all-reduce.2.cloned.1.call-done = f32[256,256]{1,0:T(8,128)} async-done(((f32[256,256]{1,0:T(8,128)}), f32[256,256]{1,0:T(8,128)}) %all-reduce.2.cloned.1.call-update) | async-done | bytes 262160 | tf_op jit(solution)/shard_map/psum | solution.py:63
  (96 shorter events, 81.1 us)
Async XLA Ops:
  7.2 241.5 %copy-start = (bf16[256,256]{1,0:T(8,128)(2,1)S(1)}, bf16[256,256]{1,0:T(8,128)(2,1)}, u32[]{:S(2)}) copy-start(bf16[256,256]{1,0:T(8,128)(2,1)} %param.12) | copy-start | bytes 393220
  7.2 45.9 %copy-start.2 = (s32[1,1,192,2]{2,3,1,0:T(2,128)S(1)}, s32[1,1,192,2]{2,3,1,0:T(2,128)}, u32[]{:S(2)}) copy-start(s32[1,1,192,2]{2,3,1,0:T(2,128)} %param.16) | copy-start | bytes 4612
  7.2 43.5 %all-gather.3.cloned.1.call-start = ((), (), s32[]{:S(2)}) async-start(), calls=%async_computation.2 | async-start | bytes 2228224 | tf_op jit(solution)/shard_map/all_gather | solution.py:50
  7.9 240.7 %reduce-scatter.3.cloned.1.call-start = ((), (), s32[]{:S(2)}) async-start(), calls=%async_computation.3 | async-start | bytes 4456448 | tf_op jit(solution)/shard_map/reduce_scatter | solution.py:54
  154.1 94.5 %copy-start.3 = (bf16[256,256]{1,0:T(8,128)(2,1)S(1)}, bf16[256,256]{1,0:T(8,128)(2,1)}, u32[]{:S(2)}) copy-start(bf16[256,256]{1,0:T(8,128)(2,1)} %param.14) | copy-start | bytes 393220
  154.1 94.5 %copy-start.4 = (f32[256]{0:T(256)S(1)}, f32[256]{0:T(256)}, u32[]{:S(2)}) copy-start(f32[256]{0:T(256)} %param.13) | copy-start | bytes 3076
  154.2 155.4 %all-gather.5.cloned.1.call-start = ((), (), s32[]{:S(2)}) async-start(), calls=%async_computation.5 | async-start | bytes 2228224 | tf_op jit(solution)/shard_map/all_gather | solution.py:59
  251.4 240.6 %reduce-scatter.5.cloned.1.call-start = ((), (), s32[]{:S(2)}) async-start(), calls=%async_computation.6 | async-start | bytes 4456448 | tf_op jit(solution)/shard_map/reduce_scatter | solution.py:64
  413.3 0.9 copy-start.1
  413.3 325.5 %all-reduce.2.cloned.1.call-start = ((), (), s32[]{:S(2)}) async-start(), calls=%async_computation.4 | async-start | bytes 524288 | tf_op jit(solution)/shard_map/psum | solution.py:63
Sparse Core Ops, SparseCore 0:
  9.9 40.7 all-gather.2
  154.3 94.2 reduce-scatter.2
  251.9 57.5 all-gather.4
  413.5 68.4 reduce-scatter.4
  488.7 250.0 all-reduce.1
where the time goes:
time: 749 us; the launch traced here: 747 us
  waiting for transfers between devices  432 us (58%)
  other arithmetic  129 us (17%)
  blocking collectives  76.8 us (10%)
  matrix products  50.5 us (7%)
  local copies, waits for them, and re-layouts  44.4 us (6%)
  between operations  13.8 us (2%)
    psum x1, waiting for transfers between devices, body(): weight_grad, bias_grad = lax.psum((weight_part, bias_part), ('row', 'col'))  245 us
    scatter-add x12, other arithmetic, step(): return acc.at[where_at[:, write_at]].add(product)  119 us
    reduce_scatter x1, waiting for transfers between devices, body(): lax.psum_scatter(partial_value, 'col', scatter_dimension=0, tiled=True)  94.4 us
    psum x1, blocking collectives, body(): weight_grad, bias_grad = lax.psum((weight_part, bias_part), ('row', 'col'))  76.8 us
    all_gather x1, waiting for transfers between devices, body(): row_grad = lax.all_gather(agg_grad, 'col', axis=0, tiled=True)  49.4 us
    dot_general x12, matrix products, step(): product = jnp.einsum(form, piece, taken, preferred_element_type=jnp.float32)  46.8 us
    all_gather x1, waiting for transfers between devices, body(): column_feats = lax.all_gather(node_feats, 'row', axis=0, tiled=True)  42.7 us
    gather x12, local copies, waits for them, and re-layouts, step(): taken = src_tiles[where_at[:, read_at]]  27.2 us
  transfers between devices with their start and end apart: 5, of which 4 were waited for; matrix products, arithmetic and copies ran while one was open for 1% of the time, Pallas kernels for 0%

commit v1 on v0

v1 whole, which is shorter than its diff:
```python
import functools

import jax
import jax.numpy as jnp
from jax import lax
from jax.experimental import pallas as pl
from jax.experimental.pallas import tpu as pltpu
from jax.sharding import PartitionSpec as P

F = 256
H = 128
T = 128
SLOTS = 192
TR = 32
BF = jnp.bfloat16
F32 = jnp.float32
MESH = pl.DeviceIdType.MESH
UNROLL = 16
WR = 24


def slot_order(coords_ref, count, meta):
    slot = lax.broadcasted_iota(jnp.int32, (SLOTS, 1), 0)
    lane = lax.broadcasted_iota(jnp.int32, (SLOTS, 256), 1)
    sub = lax.broadcasted_iota(jnp.int32, (SLOTS, 256), 0)
    rows = coords_ref[:, 0:1]
    cols = coords_ref[:, 1:2]
    live = slot < count
    value = slot + rows * 256 + cols * 8192
    for at, (major, minor) in enumerate(((rows, cols), (cols, rows))):
        key = jnp.where(live, major * TR + minor, TR * TR + slot)
        across = jnp.sum(jnp.where(sub == lane, key, 0), axis=0, keepdims=True)
        less = jnp.logical_and(across < key, lane < SLOTS)
        rank = jnp.sum(jnp.where(less, 1, 0), axis=1, keepdims=True)
        meta[at : at + 1, :] = jnp.sum(jnp.where(rank == lane, value, 0), axis=0, keepdims=True)
        upto = jnp.logical_and(major <= lane, live)
        meta[at + 2 : at + 3, :] = jnp.sum(jnp.where(upto, 1, 0), axis=0, keepdims=True) - 1


def tile_sums(order, tiles, source, prefix, out, back):
    def place(slot):
        word = order[1 if back else 0, slot]
        index = lax.rem(word, 256)
        row = lax.rem(lax.div(word, 256), TR)
        col = lax.div(word, 8192)
        return (index, col, row) if back else (index, row, col)

    def product(index, read):
        dims = (((0,), (0,)), ((), ())) if back else (((1,), (0,)), ((), ()))
        return lax.dot_general(tiles[index], source[read], dims, preferred_element_type=F32)

    def step(block, acc):
        start = block * UNROLL
        places = [place(start + u) for u in range(UNROLL)]
        before = place(jnp.maximum(start - 1, 0))[1]
        products = [product(index, read) for index, _, read in places]
        for u in range(UNROLL):
            write = places[u][1]
            acc = jnp.where(write == before, acc, 0.0) + products[u]
            prefix[start + u] = acc.astype(BF)
            before = write
        return acc

    lax.fori_loop(0, SLOTS // UNROLL, step, jnp.zeros((T, H), F32))

    def take(r, _):
        last = order[3 if back else 2, r]
        previous = jnp.where(r == 0, -1, order[3 if back else 2, jnp.maximum(r - 1, 0)])
        value = prefix[jnp.maximum(last, 0)]
        out[r] = jnp.where(last > previous, value, jnp.zeros_like(value))
        return 0

    lax.fori_loop(0, TR, take, 0, unroll=4)


def kernel(
    feats_in, weight, bias, cotangent, tiles_hbm, coords, counts,
    activations, weight_grad, bias_grad, feats_grad,
    tiles, meta, order, prefix, f0, f1, s0, s1, x0, x1, zs0, zs1, zr0, zr1, own0, own1, agg, g0, g1,
    cr0, cr1, rs0, rs1, rr0, rr1, ws, wx, wzs, wz, wcs, wcr, wrs, wr, wout,
    local_sem, f_send, f_recv, fc_send, fc_recv, x_send, x_recv, z_send, z_recv,
    gz_send, gz_recv, gx_send, gx_recv, c_send, c_recv, r_send, r_recv,
    wx_send, wx_recv, wz_send, wz_recv, wc_send, wc_recv, wr_send, wr_recv,
    va_send, va_recv, vb_send, vb_recv,
):
    row, col = lax.axis_index("row"), lax.axis_index("col")
    y, zl, core = lax.div(row, 4), lax.rem(lax.div(row, 2), 2), lax.rem(row, 2)
    zh, x = lax.div(col, 4), lax.rem(col, 4)

    def row_at(dy, dz, dc):
        return (lax.rem(y + dy, 4) * 2 + lax.rem(zl + dz, 2)) * 2 + lax.rem(core + dc, 2)

    def col_at(dz, dx):
        return lax.rem(zh + dz, 4) * 4 + lax.rem(x + dx, 4)

    sibling = (row_at(0, 0, 1), col)
    chips = [(dy, dz) for dy in range(4) for dz in range(2) if (dy, dz) != (0, 0)]
    sends = []

    def send(src, dst, ssem, rsem, device):
        copy = pltpu.make_async_remote_copy(
            src_ref=src, dst_ref=dst, send_sem=ssem, recv_sem=rsem, device_id=device, device_id_type=MESH
        )
        copy.start()
        sends.append(copy)
        return copy

    load = pltpu.make_async_copy(tiles_hbm, tiles, local_sem.at[0])
    load.start()

    partners = [sibling]
    partners += [(row_at(dy, dz, 0), col) for dy, dz in chips]
    partners += [(row, col_at(0, d)) for d in range(1, 4)]
    partners += [(row, col_at(d, 0)) for d in range(1, 4)]
    barrier = pltpu.get_barrier_semaphore()
    for device in partners:
        pl.semaphore_signal(barrier, inc=1, device_id=device, device_id_type=MESH)
    feats = (f0, f1)
    for h in range(2):
        feats[h][pl.ds(2 * row, 2)] = feats_in[:, h * H : (h + 1) * H].reshape(2, T, H)
    pl.semaphore_wait(barrier, len(partners))

    got = {}
    for h in range(2):
        mine = feats[h].at[pl.ds(2 * row, 2)]
        for n, (dy, dz) in enumerate(chips):
            got[h, n] = send(mine, mine, f_send.at[h, n], f_recv.at[h, n], (row_at(dy, dz, 0), col))
        got[h, 7] = send(mine, mine, fc_send.at[h, 7], fc_recv.at[h, 7], sibling)

    slot_order(coords, counts[0, 0], meta)
    move = pltpu.make_async_copy(meta, order, local_sem.at[1])
    move.start()
    move.wait()
    load.wait()

    sums = (s0, s1)
    xr = (x0, x1)
    zsend = (zs0, zs1)
    zrecv = (zr0, zr1)
    own = (own0, own1)

    def gather_features(h):
        passed = []
        for n, (dy, dz) in enumerate(chips):
            got[h, n].wait_recv()
            came = feats[h].at[pl.ds(2 * row_at(4 - dy, dz, 0), 2)]
            passed.append(send(came, came, fc_send.at[h, n], fc_recv.at[h, n], sibling))
        got[h, 7].wait_recv()
        for copy in passed:
            copy.wait_recv()

    xcopies = {}

    def scatter_x(h):
        for k in (2, 1, 3, 0):
            for d in (2, 1, 3):
                at = pl.ds(2 * col_at(k, d), 2)
                xcopies[h, k, d] = send(
                    sums[h].at[at], xr[h].at[d - 1, k], x_send.at[h, d - 1, k], x_recv.at[h, d - 1, k],
                    (row, col_at(0, d)),
                )

    zcopies = {}

    def scatter_z(h):
        for k in (2, 1, 3, 0):
            total = sums[h][pl.ds(2 * col_at(k, 0), 2)].astype(F32)
            for d in range(1, 4):
                xcopies[h, k, d].wait_recv()
                total += xr[h][d - 1, k].astype(F32)
            if k:
                zsend[h][k - 1] = total.astype(BF)
                zcopies[h, k] = send(
                    zsend[h].at[k - 1], zrecv[h].at[k - 1], z_send.at[h, k - 1], z_recv.at[h, k - 1],
                    (row, col_at(k, 0)),
                )
            else:
                own[h][...] = total

    def finish_aggregate(h):
        total = own[h][...]
        for k in range(1, 4):
            zcopies[h, k].wait_recv()
            total += zrecv[h][k - 1].astype(F32)
        agg[:, h * H : (h + 1) * H] = total.reshape(2 * T, H).astype(BF)

    gather_features(0)
    tile_sums(order, tiles, f0, prefix, s0, False)
    scatter_x(0)
    gather_features(1)
    tile_sums(order, tiles, f1, prefix, s1, False)
    scatter_x(1)
    scatter_z(0)
    scatter_z(1)
    finish_aggregate(0)
    finish_aggregate(1)

    pre = jnp.dot(agg[...], weight[...], preferred_element_type=F32) + bias[...]
    gate = jax.nn.sigmoid(pre)
    pre_grad = (cotangent[...].astype(F32) * gate * (1.0 + pre * (1.0 - gate))).astype(BF)
    agg_grad = lax.dot_general(
        pre_grad, weight[...], (((1,), (1,)), ((), ())), preferred_element_type=F32
    ).astype(BF)
    grads = (g0, g1)
    for h in range(2):
        grads[h][pl.ds(2 * col, 2)] = agg_grad[:, h * H : (h + 1) * H].reshape(2, T, H)

    gz = {}
    gx = {}

    def spread_x(h, k):
        came = grads[h].at[pl.ds(2 * col_at(4 - k if k else 0, 0), 2)]
        for d in (2, 1, 3):
            gx[h, k, d] = send(
                came, came, gx_send.at[h, k, d - 1], gx_recv.at[h, k, d - 1], (row, col_at(0, d))
            )

    for h in range(2):
        mine = grads[h].at[pl.ds(2 * col, 2)]
        for k in (2, 1, 3):
            gz[h, k] = send(mine, mine, gz_send.at[h, k - 1], gz_recv.at[h, k - 1], (row, col_at(k, 0)))
        spread_x(h, 0)

    activations[...] = (pre * gate).astype(BF)
    part = lax.dot_general(agg[...], pre_grad, (((0,), (0,)), ((), ())), preferred_element_type=F32)
    bias_part = jnp.broadcast_to(jnp.sum(pre_grad.astype(F32), axis=0, keepdims=True), (8, F))
    for a in range(4):
        for b in range(4):
            ws[a, b, 0:16, :] = part[64 * a + 16 * b : 64 * a + 16 * b + 16, :]
            ws[a, b, 16:WR, :] = bias_part

    for k in (1, 3, 2):
        gz[0, k].wait_recv()
        spread_x(0, k)
    for k in (1, 3, 2):
        gz[1, k].wait_recv()
        spread_x(1, k)

    wxc = [
        send(ws.at[lax.rem(x + d, 4)], wx.at[x], wx_send.at[d - 1], wx_recv.at[d - 1], (row, col_at(0, d)))
        for d in range(1, 4)
    ]
    wx[x] = ws[x]

    def gathered(h):
        for k in range(4):
            for d in range(1, 4):
                gx[h, k, d].wait_recv()

    cr = (cr0, cr1)
    rsend = (rs0, rs1)
    rrecv = (rr0, rr1)
    ccopies = {}
    rcopies = {}
    order_out = [(2, 1), (2, 0), (1, 1), (3, 1), (1, 0), (3, 0), (0, 1), (0, 0)]

    def scatter_core(h):
        for n, (dy, dz) in enumerate(order_out):
            at = pl.ds(2 * row_at(dy, dz, 1), 2)
            ccopies[h, n] = send(sums[h].at[at], cr[h].at[n], c_send.at[h, n], c_recv.at[h, n], sibling)

    def scatter_row(h):
        for n, (dy, dz) in enumerate(order_out):
            ccopies[h, n].wait_recv()
            total = sums[h][pl.ds(2 * row_at(dy, dz, 0), 2)].astype(F32) + cr[h][n].astype(F32)
            if n < 7:
                rsend[h][n] = total.astype(BF)
                rcopies[h, n] = send(
                    rsend[h].at[n], rrecv[h].at[n], r_send.at[h, n], r_recv.at[h, n], (row_at(dy, dz, 0), col)
                )
            else:
                own[h][...] = total

    def finish_feats(h):
        total = own[h][...]
        for n in range(7):
            rcopies[h, n].wait_recv()
            total += rrecv[h][n].astype(F32)
        feats_grad[:, h * H : (h + 1) * H] = total.reshape(2 * T, H).astype(BF)

    for copy in xcopies.values():
        copy.wait_send()
    early = {id(copy) for copy in xcopies.values()}

    gathered(0)
    tile_sums(order, tiles, g0, prefix, s0, True)
    scatter_core(0)

    for copy in wxc:
        copy.wait_recv()
    wzs[...] = ((wx[0] + wx[1]) + wx[2]) + wx[3]
    wzc = [
        send(wzs.at[lax.rem(zh + k, 4)], wz.at[zh], wz_send.at[k - 1], wz_recv.at[k - 1], (row, col_at(k, 0)))
        for k in range(1, 4)
    ]
    wz[zh] = wzs[zh]
    scatter_row(0)

    gathered(1)
    tile_sums(order, tiles, g1, prefix, s1, True)
    scatter_core(1)

    for copy in wzc:
        copy.wait_recv()
    wcs[...] = ((wz[0] + wz[1]) + wz[2]) + wz[3]
    wcc = send(wcs, wcr, wc_send.at[0], wc_recv.at[0], sibling)
    scatter_row(1)
    wcc.wait_recv()
    chip = y * 2 + zl
    wrs[...] = wcs[...] + wcr[...]
    wrc = [
        send(wrs, wr.at[chip], wr_send.at[n], wr_recv.at[n], (row_at(dy, dz, 0), col))
        for n, (dy, dz) in enumerate(chips)
    ]
    wr[chip] = wrs[...]
    finish_feats(0)
    for copy in wrc:
        copy.wait_recv()
    total = wr[0]
    for n in range(1, 8):
        total += wr[n]
    bias_grad[...] = total[16:17, :]
    wout[x, zh] = total[0:16, :]
    vac = [
        send(wout.at[x, zh], wout.at[x, zh], va_send.at[k - 1], va_recv.at[k - 1], (row, col_at(k, 0)))
        for k in range(1, 4)
    ]
    finish_feats(1)
    for copy in vac:
        copy.wait_recv()
    vbc = [
        send(wout.at[x], wout.at[x], vb_send.at[d - 1], vb_recv.at[d - 1], (row, col_at(0, d)))
        for d in range(1, 4)
    ]
    for copy in vbc:
        copy.wait_recv()
    weight_grad[...] = wout[...].reshape(F, F)
    for copy in sends:
        if id(copy) not in early:
            copy.wait_send()


def body(node_feats, weight, bias, cotangent, tiles, coords, counts):
    vmem = pl.BlockSpec(memory_space=pltpu.VMEM)
    half = (TR, T, H)
    dma = pltpu.SemaphoreType.DMA
    pair = lambda shape, dtype=BF: [pltpu.VMEM(shape, dtype)] * 2
    both = lambda shape: [dma(shape), dma(shape)]
    activations, weight_grad, bias_grad, feats_grad = pl.pallas_call(
        kernel,
        out_shape=(
            jax.ShapeDtypeStruct((2 * T, F), BF),
            jax.ShapeDtypeStruct((F, F), F32),
            jax.ShapeDtypeStruct((1, F), F32),
            jax.ShapeDtypeStruct((2 * T, F), BF),
        ),
        in_specs=[vmem, vmem, vmem, vmem, pl.BlockSpec(memory_space=pl.ANY), vmem,
                  pl.BlockSpec(memory_space=pltpu.SMEM)],
        out_specs=(vmem, vmem, vmem, vmem),
        scratch_shapes=[
            pltpu.VMEM((SLOTS, T, T), BF),
            pltpu.VMEM((8, 256), jnp.int32),
            pltpu.SMEM((8, 256), jnp.int32),
            pltpu.VMEM((SLOTS, T, H), BF),
            *pair(half),
            *pair(half),
            *pair((3, 4, 2, T, H)),
            *pair((3, 2, T, H)),
            *pair((3, 2, T, H)),
            *pair((2, T, H), F32),
            pltpu.VMEM((2 * T, F), BF),
            *pair(half),
            *pair((8, 2, T, H)),
            *pair((7, 2, T, H)),
            *pair((7, 2, T, H)),
            pltpu.VMEM((4, 4, WR, F), F32),
            pltpu.VMEM((4, 4, WR, F), F32),
            pltpu.VMEM((4, WR, F), F32),
            pltpu.VMEM((4, WR, F), F32),
            pltpu.VMEM((WR, F), F32),
            pltpu.VMEM((WR, F), F32),
            pltpu.VMEM((WR, F), F32),
            pltpu.VMEM((8, WR, F), F32),
            pltpu.VMEM((4, 4, 16, F), F32),
            dma((2,)),
            *both((2, 7)),
            *both((2, 8)),
            *both((2, 3, 4)),
            *both((2, 3)),
            *both((2, 3)),
            *both((2, 4, 3)),
            *both((2, 8)),
            *both((2, 7)),
            *both((3,)),
            *both((3,)),
            *both((1,)),
            *both((7,)),
            *both((3,)),
            *both((3,)),
        ],
        compiler_params=pltpu.CompilerParams(
            collective_id=0, has_side_effects=True, vmem_limit_bytes=48 * 2**20
        ),
    )(node_feats, weight, bias.reshape(1, F), cotangent, tiles.reshape(SLOTS, T, T),
      coords.reshape(SLOTS, 2), counts)
    return activations, weight_grad, bias_grad.reshape(F), feats_grad


def solution(mesh):
    return jax.shard_map(
        body,
        mesh=mesh,
        in_specs=(
            P(("col", "row"), None),
            P(),
            P(),
            P(("row", "col"), None),
            P("row", "col", None, None, None),
            P("row", "col", None, None),
            P("row", "col"),
        ),
        out_specs=(P(("row", "col"), None), P(), P(), P(("col", "row"), None)),
        check_vma=False,
    )
```

time: 749 us -> 122 us (0.16)
  the two profiles are of different devices: /device:TPU:1 before, /device:TPU:32 now
where the time goes in v1:
time: 122 us
  Pallas kernels  114 us (93%)
  local copies, waits for them, and re-layouts  6.76 us (6%)
  between operations  1.31 us (1%)
    pallas_call x1, Pallas kernels, body(): pl.pallas_call(kernel, out_shape=(jax.ShapeDtypeStruct((2 * T, F), BF), j...  114 us
    unnamed x13, local copies, waits for them, and re-layouts  6.76 us

profile of v1, /device:TPU:32, one launch (start us, length us, event | category | flops | bytes accessed | tf_op | source)
XLA Modules:
  0.0 121.9 jit_solution(11099941363410765916)
XLA Ops:
  1.3 0.8 copy.11
  2.1 0.0 copy-start
  2.1 0.9 copy-done
  3.0 0.0 copy-start.1
  3.0 0.9 copy-done.1
  3.9 0.0 copy-start.2
  3.9 0.9 copy-done.2
  4.8 0.0 copy-start.3
  4.8 0.7 copy-done.3
  5.5 113.8 %shard_map.102 = (bf16[256,256]{1,0:T(8,128)(2,1)S(1)}, f32[256,256]{1,0:T(8,128)S(1)}, f32[1,256]{1,0:T(1,128)S(1)}, bf16[256,256]{1,0:T(8,128)(2,1)S(1)}) custom-call(bf16[256,256]{1,0:T(8,128)(2,1)S(1)} %copy-done, bf16[256,256]{1,0:T(8,128)(2,1)S(1)} %copy-done.1, f32[1,256]{1,0:T(1,128)S(1)} %bitcast.5, bf16[256,256]{1,0:T(8,128)(2,1)S(1)} %copy-done.2, ...), custom_call_target="tpu_custom_call" | custom-call | tf_op jit(solution)/shard_map/pallas_call | solution.py:349
  119.3 0.7 copy.17
  119.9 0.7 copy.18
  120.6 0.6 copy.19
  121.2 0.7 copy.20
Async XLA Ops:
  2.1 0.9 copy-start
  3.0 0.9 copy-start.1
  3.9 0.9 copy-start.2
  4.8 0.7 copy-start.3

commit v2 on v1

v2 whole, which is shorter than its diff:
```python
import functools

import jax
import jax.numpy as jnp
from jax import lax
from jax.experimental import pallas as pl
from jax.experimental.pallas import tpu as pltpu
from jax.sharding import PartitionSpec as P

F = 256
H = 128
T = 128
SLOTS = 192
TR = 32
BF = jnp.bfloat16
F32 = jnp.float32
MESH = pl.DeviceIdType.MESH
UNROLL = 16


class Sent:
    def __init__(self, copy):
        self.copy, self.here, self.there = copy, False, False

    def wait_recv(self):
        if not self.here:
            self.copy.wait_recv()
        self.here = True

    def wait(self):
        if not self.here:
            self.copy.wait()
        self.here = True

    def wait_send(self):
        if not self.there:
            self.copy.wait_send()
        self.there = True


def slot_order(coords_ref, count, meta):
    lane = lax.broadcasted_iota(jnp.int32, (SLOTS, SLOTS), 1)
    sub = lax.broadcasted_iota(jnp.int32, (SLOTS, SLOTS), 0)
    slot = lax.broadcasted_iota(jnp.int32, (SLOTS, 1), 0)
    across_slot = lax.broadcasted_iota(jnp.int32, (1, SLOTS), 1)

    def down(across):
        return jnp.sum(jnp.where(sub == lane, across, 0), axis=1, keepdims=True)

    rows, cols = coords_ref[0:1, :], coords_ref[1:2, :]
    rows_down, cols_down = down(rows), down(cols)
    live, live_down = across_slot < count, slot < count
    value = slot + rows_down * 256 + cols_down * 8192
    for at, (major, minor, major_down, minor_down) in enumerate(
        ((rows, cols, rows_down, cols_down), (cols, rows, cols_down, rows_down))
    ):
        key = jnp.where(live, major * TR + minor, TR * TR + across_slot)
        key_down = jnp.where(live_down, major_down * TR + minor_down, TR * TR + slot)
        rank = jnp.sum(jnp.where(key < key_down, 1, 0), axis=1, keepdims=True)
        meta[at : at + 1, 0:SLOTS] = jnp.sum(jnp.where(rank == lane, value, 0), axis=0, keepdims=True)
        upto = jnp.logical_and(major_down <= lane, live_down)
        meta[at + 2 : at + 3, 0:SLOTS] = jnp.sum(jnp.where(upto, 1, 0), axis=0, keepdims=True) - 1


def tile_sums(order, tiles, source, prefix, back, between=()):
    def place(slot):
        word = order[1 if back else 0, slot]
        index = word & 255
        row = lax.shift_right_logical(word, 8) & (TR - 1)
        col = lax.shift_right_logical(word, 13)
        return (index, col, row) if back else (index, row, col)

    def product(index, read):
        dims = (((0,), (0,)), ((), ())) if back else (((1,), (0,)), ((), ()))
        return lax.dot_general(tiles[index], source[read], dims, preferred_element_type=F32)

    def step(block, acc):
        start = block * UNROLL
        places = [place(start + u) for u in range(UNROLL)]
        before = place(jnp.maximum(start - 1, 0))[1]
        products = [product(index, read) for index, _, read in places]
        for u in range(UNROLL):
            write = places[u][1]
            acc = jnp.where(write == before, acc, 0.0) + products[u]
            prefix[start + u] = acc.astype(BF)
            before = write
        return acc

    steps, parts = SLOTS // UNROLL, len(between) + 1
    acc = jnp.zeros((T, H), F32)
    for n in range(parts):
        acc = lax.fori_loop(steps * n // parts, steps * (n + 1) // parts, step, acc)
        if n < len(between):
            between[n]()


def take(order, prefix, out, block, back):
    line = 3 if back else 2
    for u in range(2):
        r = 2 * block + u
        last = order[line, r]
        previous = jnp.where(r == 0, -1, order[line, jnp.maximum(r - 1, 0)])
        value = prefix[jnp.maximum(last, 0)]
        out[r] = jnp.where(last > previous, value, jnp.zeros_like(value))


def kernel(
    feats_hbm, weight_hbm, bias_hbm, cotangent_hbm, tiles_hbm, coords_hbm, counts,
    activations, weight_grad, bias_grad, feats_grad,
    feats_in, weight, bias, cotangent, coords,
    tiles, meta, order, p0, p1, f0, f1, s0, s1, u0, u1, xb0, xb1, xc0, xc1, xp0, xp1,
    zs0, zs1, zr0, zr1, own0, own1, agg, g0, g1,
    cr0, cr1, rs0, rs1, rr0, rr1, ws, wc, wy, ws2, wx, ws3, wl, ws4, wz, wout,
    local_sem, f_send, f_recv, fc_send, fc_recv, x_send, x_recv, z_send, z_recv,
    gz_send, gz_recv, gx_send, gx_recv, c_send, c_recv, r_send, r_recv, w_send, w_recv,
):
    row, col = lax.axis_index("row"), lax.axis_index("col")
    y, zl, core = lax.div(row, 4), lax.rem(lax.div(row, 2), 2), lax.rem(row, 2)
    zh, x = lax.div(col, 4), lax.rem(col, 4)
    side = 1 + 2 * core

    def row_at(dy, dz, dc):
        return (lax.rem(y + dy, 4) * 2 + lax.rem(zl + dz, 2)) * 2 + lax.rem(core + dc, 2)

    def col_at(dz, dx):
        return lax.rem(zh + dz, 4) * 4 + lax.rem(x + dx, 4)

    sibling = (row_at(0, 0, 1), col)
    ahead, behind = (row, col_at(0, side)), (row, col_at(0, 4 - side))
    chips = [(2, 1), (2, 0), (1, 1), (3, 1), (1, 0), (3, 0), (0, 1)]
    sends = []
    locals_ = []

    def send(src, dst, ssem, rsem, device):
        copy = pltpu.make_async_remote_copy(
            src_ref=src, dst_ref=dst, send_sem=ssem, recv_sem=rsem, device_id=device, device_id_type=MESH
        )
        copy.start()
        copy = Sent(copy)
        sends.append(copy)
        return copy

    def load(src, dst):
        copy = pltpu.make_async_copy(src, dst, local_sem.at[len(locals_)])
        copy.start()
        copy = Sent(copy)
        locals_.append(copy)
        return copy

    partners = [sibling]
    partners += [(row_at(dy, dz, 0), col) for dy, dz in chips]
    partners += [(row, col_at(0, d)) for d in range(1, 4)]
    partners += [(row, col_at(d, 0)) for d in range(1, 4)]
    barrier = pltpu.get_barrier_semaphore()
    for device in partners:
        pl.semaphore_signal(barrier, inc=1, device_id=device, device_id_type=MESH)
    load_feats = load(feats_hbm, feats_in)
    load_coords = load(coords_hbm, coords)
    load_tiles = load(tiles_hbm, tiles)
    load_dense = [load(weight_hbm, weight), load(bias_hbm, bias), load(cotangent_hbm, cotangent)]
    feats = (f0, f1)
    load_feats.wait()
    for h in range(2):
        feats[h][pl.ds(2 * row, 2)] = feats_in[:, h * H : (h + 1) * H].reshape(2, T, H)
    pl.semaphore_wait(barrier, len(partners))

    got = {}

    def send_features(h):
        mine = feats[h].at[pl.ds(2 * row, 2)]
        for n, (dy, dz) in enumerate(chips):
            got[h, n] = send(mine, mine, f_send.at[h, n], f_recv.at[h, n], (row_at(dy, dz, 0), col))
        got[h, 7] = send(mine, mine, fc_send.at[h, 7], fc_recv.at[h, 7], sibling)

    send_features(0)
    load_coords.wait()
    slot_order(coords, counts[0, 0], meta)
    load_order = load(meta, order)
    load_order.wait()
    load_tiles.wait()
    for copy in load_dense:
        copy.wait()

    sums = (s0, s1)
    prefix = (p0, p1)
    relay, combined, plain, summed = (u0, u1), (xb0, xb1), (xc0, xc1), (xp0, xp1)
    zsend = (zs0, zs1)
    zrecv = (zr0, zr1)
    own = (own0, own1)
    places = (2, 1, 3, 0)

    def gather_features(h, early=None):
        passed = []
        for at, n in enumerate((4, 5, 6, 2, 3, 1, 0)):
            dy, dz = chips[n]
            got[h, n].wait_recv()
            came = feats[h].at[pl.ds(2 * row_at(4 - dy, dz, 0), 2)]
            passed.append(send(came, came, fc_send.at[h, n], fc_recv.at[h, n], sibling))
            if early and at == 2:
                early()
        got[h, 7].wait_recv()
        for copy in passed:
            copy.wait_recv()

    xcopies = {}

    def send_sum(h, k, kind, src, dst, device):
        xcopies[h, k, kind] = send(src, dst, x_send.at[h, kind, k], x_recv.at[h, kind, k], device)

    def scatter_far(h, k):
        for kind, d, dst, device in ((0, 2, relay, ahead), (1, 4 - side, plain, behind)):
            block = col_at(k, d)
            take(order, prefix[h], sums[h], block, False)
            send_sum(h, k, kind, sums[h].at[pl.ds(2 * block, 2)], dst[h].at[k], device)

    def scatter_ahead(h, k):
        block = col_at(k, side)
        take(order, prefix[h], sums[h], block, False)
        xcopies[h, k, 0].wait_recv()
        mine = sums[h][pl.ds(2 * block, 2)]
        summed[h][k] = (mine.astype(F32) + relay[h][k].astype(F32)).astype(BF)
        send_sum(h, k, 2, summed[h].at[k], combined[h].at[k], ahead)

    zcopies = {}

    def scatter_z(h, k):
        block = col_at(k, 0)
        take(order, prefix[h], sums[h], block, False)
        xcopies[h, k, 1].wait_recv()
        xcopies[h, k, 2].wait_recv()
        total = sums[h][pl.ds(2 * block, 2)].astype(F32)
        total += plain[h][k].astype(F32) + combined[h][k].astype(F32)
        if k:
            zsend[h][k - 1] = total.astype(BF)
            zcopies[h, k] = send(
                zsend[h].at[k - 1], zrecv[h].at[k - 1], z_send.at[h, k - 1], z_recv.at[h, k - 1],
                (row, col_at(k, 0)),
            )
        else:
            own[h][...] = total

    def finish_aggregate(h):
        total = own[h][...]
        for k in range(1, 4):
            zcopies[h, k].wait_recv()
            total += zrecv[h][k - 1].astype(F32)
        agg[:, h * H : (h + 1) * H] = total.reshape(2 * T, H).astype(BF)

    units = [(h, k) for h in range(2) for k in (2, 1, 3, 0)]
    gather_features(0, lambda: send_features(1))
    tile_sums(order, tiles, f0, p0, False)
    scatter_far(*units[0])
    scatter_far(*units[1])
    gather_features(1)
    scatter_ahead(*units[0])
    scatter_far(*units[2])
    scatter_far(*units[3])
    tile_sums(order, tiles, f1, p1, False)
    for n in range(4, 12):
        if n < 8:
            scatter_far(*units[n])
        if n == 4:
            scatter_ahead(*units[1])
        if n < 10:
            scatter_ahead(*units[n - 2])
        if n >= 5:
            scatter_z(*units[n - 5])
    scatter_z(*units[7])
    finish_aggregate(0)
    finish_aggregate(1)

    pre = jnp.dot(agg[...], weight[...], preferred_element_type=F32) + bias[...]
    gate = jax.nn.sigmoid(pre)
    pre_grad = (cotangent[...].astype(F32) * gate * (1.0 + pre * (1.0 - gate))).astype(BF)
    agg_grad = lax.dot_general(
        pre_grad, weight[...], (((1,), (1,)), ((), ())), preferred_element_type=F32
    ).astype(BF)
    grads = (g0, g1)
    for h in range(2):
        grads[h][pl.ds(2 * col, 2)] = agg_grad[:, h * H : (h + 1) * H].reshape(2, T, H)

    gz = {}
    gx = {}

    def origin(k, d):
        return grads_at(col_at(4 - k if k else 0, d))

    def grads_at(block):
        return pl.ds(2 * block, 2)

    def spread(h, k):
        came = grads[h].at[origin(k, 0)]
        gx[h, k, 0] = send(came, came, gx_send.at[h, k, 0], gx_recv.at[h, k, 0], ahead)
        gx[h, k, 1] = send(came, came, gx_send.at[h, k, 1], gx_recv.at[h, k, 1], behind)

    def pass_on(h, k):
        gx[h, k, 0].wait_recv()
        came = grads[h].at[origin(k, 4 - side)]
        gx[h, k, 2] = send(came, came, gx_send.at[h, k, 2], gx_recv.at[h, k, 2], ahead)

    def spread_z(h, k):
        mine = grads[h].at[pl.ds(2 * col, 2)]
        gz[h, k] = send(mine, mine, gz_send.at[h, k - 1], gz_recv.at[h, k - 1], (row, col_at(k, 0)))

    def came_z(h, k):
        gz[h, k].wait_recv()
        spread(h, k)

    spread_z(0, 1)
    spread_z(0, 3)
    spread(0, 0)
    spread(1, 0)

    activations[...] = (pre * gate).astype(BF)
    part = lax.dot_general(agg[...], pre_grad, (((0,), (0,)), ((), ())), preferred_element_type=F32)
    bias_part = jnp.broadcast_to(jnp.sum(pre_grad.astype(F32), axis=0, keepdims=True), (8, F))
    for n in range(32):
        ws[n // 16, n // 4 % 4, n % 4, 0:8, :] = part[8 * n : 8 * n + 8, :]
        ws[n // 16, n // 4 % 4, n % 4, 8:16, :] = bias_part
    stage = {}
    wnext = [0]

    def wsend(name, src, dst, device):
        n = wnext[0]
        wnext[0] += 1
        stage.setdefault(name, []).append(send(src, dst, w_send.at[n], w_recv.at[n], device))

    def landed(name):
        for copy in stage[name]:
            copy.wait_recv()

    def along_y(d):
        return (row_at(d, 0, 0), col)

    def along_x(d):
        return (row, col_at(0, d))

    def w_core():
        wsend("core", ws.at[1 - core], wc, sibling)

    def w_y():
        landed("core")
        for a in range(4):
            ws2[a] = ws[core, a] + wc[a]
        for d in range(1, 4):
            wsend("y", ws2.at[lax.rem(y + d, 4)], wy.at[y], along_y(d))
        wy[y] = ws2[y]

    def w_x():
        landed("y")
        ws3[...] = ((wy[0] + wy[1]) + wy[2]) + wy[3]
        for d in range(1, 4):
            wsend("x", ws3.at[lax.rem(x + d, 4)], wx.at[x], along_x(d))
        wx[x] = ws3[x]

    def w_zl():
        landed("x")
        ws4[0] = ((wx[0] + wx[1]) + wx[2]) + wx[3]
        wsend("zl", ws4.at[0], wl, (row_at(0, 1, 0), col))

    def w_zh():
        landed("zl")
        ws4[1] = ws4[0] + wl[...]
        for d in range(1, 4):
            wsend("zh", ws4.at[1], wz.at[zh], (row, col_at(d, 0)))
        wz[zh] = ws4[1]

    def v_x():
        landed("zh")
        total = ((wz[0] + wz[1]) + wz[2]) + wz[3]
        bias_grad[...] = total[8:9, :]
        wout[core, y, x] = total[0:8, :]
        at = wout.at[core, y, x]
        for d in range(1, 4):
            wsend("vx", at, at, along_x(d))

    def v_y():
        landed("vx")
        at = wout.at[core, y]
        for d in range(1, 4):
            wsend("vy", at, at, along_y(d))

    def v_core():
        landed("vy")
        at = wout.at[core]
        wsend("vcore", at, at, sibling)

    def v_end():
        landed("vcore")
        weight_grad[...] = wout[...].reshape(F, F)

    def gathered(h):
        for k in range(4):
            for d in range(3):
                gx[h, k, d].wait_recv()

    cr = (cr0, cr1)
    rsend = (rs0, rs1)
    rrecv = (rr0, rr1)
    ccopies = {}
    rcopies = {}
    order_out = chips + [(0, 0)]

    def scatter_core(h):
        for n, (dy, dz) in enumerate(order_out):
            block = row_at(dy, dz, 1)
            take(order, prefix[h], sums[h], block, True)
            at = pl.ds(2 * block, 2)
            ccopies[h, n] = send(sums[h].at[at], cr[h].at[n], c_send.at[h, n], c_recv.at[h, n], sibling)

    def scatter_row(h, at=range(8)):
        for n in at:
            dy, dz = order_out[n]
            block = row_at(dy, dz, 0)
            take(order, prefix[h], sums[h], block, True)
            ccopies[h, n].wait_recv()
            total = sums[h][pl.ds(2 * block, 2)].astype(F32) + cr[h][n].astype(F32)
            if n < 7:
                rsend[h][n] = total.astype(BF)
                rcopies[h, n] = send(
                    rsend[h].at[n], rrecv[h].at[n], r_send.at[h, n], r_recv.at[h, n], (row_at(dy, dz, 0), col)
                )
            else:
                own[h][...] = total

    def finish_feats(h):
        total = own[h][...]
        for n in range(7):
            rcopies[h, n].wait_recv()
            total += rrecv[h][n].astype(F32)
        feats_grad[:, h * H : (h + 1) * H] = total.reshape(2 * T, H).astype(BF)

    w_core()
    pass_on(0, 0)
    came_z(0, 1)
    spread_z(0, 2)
    pass_on(1, 0)
    came_z(0, 3)
    pass_on(0, 1)
    w_y()
    came_z(0, 2)
    spread_z(1, 1)
    spread_z(1, 3)
    pass_on(0, 3)
    pass_on(0, 2)
    came_z(1, 1)
    spread_z(1, 2)
    came_z(1, 3)
    w_x()
    for copy in xcopies.values():
        copy.wait_send()
    gathered(0)

    def more_1():
        pass_on(1, 1)
        came_z(1, 2)

    def more_2():
        pass_on(1, 3)
        w_zl()

    tile_sums(order, tiles, g0, p0, True, (more_1, more_2))
    pass_on(1, 2)
    scatter_core(0)
    w_zh()
    gathered(1)

    def row_1():
        scatter_row(0, range(4))
        v_x()

    def row_2():
        scatter_row(0, range(4, 8))
        v_y()

    tile_sums(order, tiles, g1, p1, True, (row_1, row_2))
    scatter_core(1)
    scatter_row(1)
    v_core()
    finish_feats(0)
    finish_feats(1)
    v_end()
    for copy in sends:
        copy.wait_send()


def copy_out(*refs):
    for n in range(4):
        refs[n + 4][...] = refs[n][...]


def body(node_feats, weight, bias, cotangent, tiles, coords, counts):
    vmem = pl.BlockSpec(memory_space=pltpu.VMEM)
    hbm = pl.BlockSpec(memory_space=pltpu.HBM)
    half = (TR, T, H)
    dma = pltpu.SemaphoreType.DMA
    pair = lambda shape, dtype=BF: [pltpu.VMEM(shape, dtype)] * 2
    both = lambda shape: [dma(shape), dma(shape)]
    outs = (
        jax.ShapeDtypeStruct((2 * T, F), BF),
        jax.ShapeDtypeStruct((F, F), F32),
        jax.ShapeDtypeStruct((1, F), F32),
        jax.ShapeDtypeStruct((2 * T, F), BF),
    )
    results = pl.pallas_call(
        kernel,
        out_shape=outs,
        in_specs=[hbm] * 6 + [pl.BlockSpec(memory_space=pltpu.SMEM)],
        out_specs=(vmem, vmem, vmem, vmem),
        scratch_shapes=[
            pltpu.VMEM((2 * T, F), BF),
            pltpu.VMEM((F, F), BF),
            pltpu.VMEM((1, F), F32),
            pltpu.VMEM((2 * T, F), BF),
            pltpu.VMEM((2, SLOTS), jnp.int32),
            pltpu.VMEM((SLOTS, T, T), BF),
            pltpu.VMEM((8, 256), jnp.int32),
            pltpu.SMEM((8, 256), jnp.int32),
            *pair((SLOTS, T, H)),
            *pair(half),
            *pair(half),
            *pair((4, 2, T, H)),
            *pair((4, 2, T, H)),
            *pair((4, 2, T, H)),
            *pair((4, 2, T, H)),
            *pair((3, 2, T, H)),
            *pair((3, 2, T, H)),
            *pair((2, T, H), F32),
            pltpu.VMEM((2 * T, F), BF),
            *pair(half),
            *pair((8, 2, T, H)),
            *pair((7, 2, T, H)),
            *pair((7, 2, T, H)),
            pltpu.VMEM((2, 4, 4, 16, F), F32),
            pltpu.VMEM((4, 4, 16, F), F32),
            pltpu.VMEM((4, 4, 16, F), F32),
            pltpu.VMEM((4, 4, 16, F), F32),
            pltpu.VMEM((4, 16, F), F32),
            pltpu.VMEM((4, 16, F), F32),
            pltpu.VMEM((16, F), F32),
            pltpu.VMEM((2, 16, F), F32),
            pltpu.VMEM((4, 16, F), F32),
            pltpu.VMEM((2, 4, 4, 8, F), F32),
            dma((7,)),
            *both((2, 7)),
            *both((2, 8)),
            *both((2, 3, 4)),
            *both((2, 3)),
            *both((2, 3)),
            *both((2, 4, 3)),
            *both((2, 8)),
            *both((2, 7)),
            *both((18,)),
        ],
        compiler_params=pltpu.CompilerParams(
            collective_id=0, has_side_effects=True, vmem_limit_bytes=63 * 2**20
        ),
    )(node_feats, weight, bias.reshape(1, F), cotangent, tiles.reshape(SLOTS, T, T),
      coords.reshape(SLOTS, 2).T, counts)
    activations, weight_grad, bias_grad, feats_grad = pl.pallas_call(
        copy_out,
        out_shape=outs,
        in_specs=[vmem] * 4,
        out_specs=[vmem] * 4,
        compiler_params=pltpu.CompilerParams(vmem_limit_bytes=63 * 2**20),
    )(*results)
    return activations, weight_grad, bias_grad.reshape(F), feats_grad


def solution(mesh):
    return jax.shard_map(
        body,
        mesh=mesh,
        in_specs=(
            P(("col", "row"), None),
            P(),
            P(),
            P(("row", "col"), None),
            P("row", "col", None, None, None),
            P("row", "col", None, None),
            P("row", "col"),
        ),
        out_specs=(P(("row", "col"), None), P(), P(), P(("col", "row"), None)),
        check_vma=False,
    )
```

time: 122 us -> 102 us (0.84)
  the two profiles are of different devices: /device:TPU:32 before, /device:TPU:1 now
where the time goes in v2:
time: 102 us
  Pallas kernels  100 us (98%)
  between operations  1.29 us (1%)
    pallas_call x1, Pallas kernels, body(): pl.pallas_call(kernel, out_shape=outs, in_specs=[hbm] * 6 + [pl.BlockSpec...  98.5 us

profile of v2, /device:TPU:1, one launch (start us, length us, event | category | flops | bytes accessed | tf_op | source)
XLA Modules:
  0.0 101.7 jit_solution(12327376899069388266)
XLA Ops:
  1.3 98.5 %shard_map.102 = (bf16[256,256]{1,0:T(8,128)(2,1)}, f32[256,256]{1,0:T(8,128)}, f32[1,256]{1,0:T(1,128)}, bf16[256,256]{1,0:T(8,128)(2,1)}) custom-call(bf16[256,256]{1,0:T(8,128)(2,1)} %feats_hbm.1, bf16[256,256]{1,0:T(8,128)(2,1)} %weight_hbm.1, f32[1,256]{1,0:T(1,128)} %bitcast.8, bf16[256,256]{1,0:T(8,128)(2,1)} %cotangent_hbm.1, ...), custom_call_target="tpu_custom_call" | custom-call | tf_op jit(solution)/shard_map/pallas_call | solution.py:505
  99.8 1.9 %shard_map.103 = (bf16[256,256]{1,0:T(8,128)(2,1)}, f32[256,256]{1,0:T(8,128)}, f32[1,256]{1,0:T(1,128)}, bf16[256,256]{1,0:T(8,128)(2,1)}) custom-call(bf16[256,256]{1,0:T(8,128)(2,1)} %get-tuple-element.12.refs_0_, f32[256,256]{1,0:T(8,128)} %get-tuple-element.13.refs_1_, f32[1,256]{1,0:T(1,128)} %get-tuple-element.14.refs_2_, ...), custom_call_target="tpu_custom_call" | custom-call | tf_op jit(solution)/shard_map/pallas_call | solution.py:560

commit v3 on v2

--- a/solution.py
+++ b/solution.py
@@ -15,7 +15,11 @@
 BF = jnp.bfloat16
 F32 = jnp.float32
 MESH = pl.DeviceIdType.MESH
-UNROLL = 16
+UNROLL = 32
+SUMS_X_STRAIGHT = frozenset(((1, 1), (1, 0)))
+SUMS_Z_STRAIGHT = frozenset((1,))
+GRADS_X_STRAIGHT = frozenset(())
+GRADS_Z_STRAIGHT = frozenset(())
 
 
 class Sent:
@@ -71,8 +75,8 @@
         return (index, col, row) if back else (index, row, col)
 
     def product(index, read):
-        dims = (((0,), (0,)), ((), ())) if back else (((1,), (0,)), ((), ()))
-        return lax.dot_general(tiles[index], source[read], dims, preferred_element_type=F32)
+        left, right = (source[read], tiles[index]) if back else (tiles[index], source[read])
+        return jnp.dot(left, right, preferred_element_type=F32)
 
     def step(block, acc):
         start = block * UNROLL
@@ -187,7 +191,9 @@
     zsend = (zs0, zs1)
     zrecv = (zr0, zr1)
     own = (own0, own1)
-    places = (2, 1, 3, 0)
+    away = (0, side, 2, 4 - side)
+    ahead_z, behind_z = (row, col_at(side, 0)), (row, col_at(4 - side, 0))
+    far, far_z = (row, col_at(0, 2)), (row, col_at(2, 0))
 
     def gather_features(h, early=None):
         passed = []
@@ -209,105 +215,131 @@
 
     def scatter_far(h, k):
         for kind, d, dst, device in ((0, 2, relay, ahead), (1, 4 - side, plain, behind)):
-            block = col_at(k, d)
+            block = col_at(away[k], d)
             take(order, prefix[h], sums[h], block, False)
+            if kind == 0 and (h, k) in SUMS_X_STRAIGHT:
+                device = far
             send_sum(h, k, kind, sums[h].at[pl.ds(2 * block, 2)], dst[h].at[k], device)
 
     def scatter_ahead(h, k):
-        block = col_at(k, side)
+        block = col_at(away[k], side)
         take(order, prefix[h], sums[h], block, False)
+        mine = pl.ds(2 * block, 2)
+        if (h, k) in SUMS_X_STRAIGHT:
+            send_sum(h, k, 2, sums[h].at[mine], combined[h].at[k], ahead)
+            return
         xcopies[h, k, 0].wait_recv()
-        mine = sums[h][pl.ds(2 * block, 2)]
-        summed[h][k] = (mine.astype(F32) + relay[h][k].astype(F32)).astype(BF)
+        summed[h][k] = (sums[h][mine].astype(F32) + relay[h][k].astype(F32)).astype(BF)
         send_sum(h, k, 2, summed[h].at[k], combined[h].at[k], ahead)
 
     zcopies = {}
 
     def scatter_z(h, k):
-        block = col_at(k, 0)
+        block = col_at(away[k], 0)
         take(order, prefix[h], sums[h], block, False)
         xcopies[h, k, 1].wait_recv()
         xcopies[h, k, 2].wait_recv()
         total = sums[h][pl.ds(2 * block, 2)].astype(F32)
         total += plain[h][k].astype(F32) + combined[h][k].astype(F32)
+        if (h, k) in SUMS_X_STRAIGHT:
+            xcopies[h, k, 0].wait_recv()
+            total += relay[h][k].astype(F32)
+        if k == 1 and h not in SUMS_Z_STRAIGHT:
+            zcopies[h, 2].wait_recv()
+            total += zrecv[h][1].astype(F32)
         if k:
             zsend[h][k - 1] = total.astype(BF)
             zcopies[h, k] = send(
                 zsend[h].at[k - 1], zrecv[h].at[k - 1], z_send.at[h, k - 1], z_recv.at[h, k - 1],
-                (row, col_at(k, 0)),
+                (ahead_z, far_z if h in SUMS_Z_STRAIGHT else ahead_z, behind_z)[k - 1],
             )
         else:
             own[h][...] = total
 
     def finish_aggregate(h):
         total = own[h][...]
-        for k in range(1, 4):
+        for k in (3, 1, 2) if h in SUMS_Z_STRAIGHT else (3, 1):
             zcopies[h, k].wait_recv()
             total += zrecv[h][k - 1].astype(F32)
         agg[:, h * H : (h + 1) * H] = total.reshape(2 * T, H).astype(BF)
 
-    units = [(h, k) for h in range(2) for k in (2, 1, 3, 0)]
     gather_features(0, lambda: send_features(1))
     tile_sums(order, tiles, f0, p0, False)
-    scatter_far(*units[0])
-    scatter_far(*units[1])
+    scatter_far(0, 2)
+    scatter_far(0, 3)
+    scatter_ahead(0, 2)
     gather_features(1)
-    scatter_ahead(*units[0])
-    scatter_far(*units[2])
-    scatter_far(*units[3])
-    tile_sums(order, tiles, f1, p1, False)
-    for n in range(4, 12):
-        if n < 8:
-            scatter_far(*units[n])
-        if n == 4:
-            scatter_ahead(*units[1])
-        if n < 10:
-            scatter_ahead(*units[n - 2])
-        if n >= 5:
-            scatter_z(*units[n - 5])
-    scatter_z(*units[7])
+    scatter_far(0, 1)
+    scatter_far(0, 0)
+    scatter_ahead(0, 3)
+    tile_sums(order, tiles, f1, p1, False, (lambda: scatter_z(0, 2),))
+    scatter_far(1, 2)
+    scatter_ahead(0, 1)
+    scatter_ahead(0, 0)
+    scatter_z(0, 3)
+    scatter_far(1, 3)
+    scatter_z(0, 1)
+    scatter_far(1, 1)
+    scatter_ahead(1, 2)
+    scatter_z(0, 0)
+    scatter_ahead(1, 3)
+    scatter_far(1, 0)
+    scatter_z(1, 2)
+    scatter_ahead(1, 1)
+    scatter_z(1, 3)
+    scatter_ahead(1, 0)
+    scatter_z(1, 1)
+    scatter_z(1, 0)
     finish_aggregate(0)
     finish_aggregate(1)
 
     pre = jnp.dot(agg[...], weight[...], preferred_element_type=F32) + bias[...]
     gate = jax.nn.sigmoid(pre)
     pre_grad = (cotangent[...].astype(F32) * gate * (1.0 + pre * (1.0 - gate))).astype(BF)
-    agg_grad = lax.dot_general(
-        pre_grad, weight[...], (((1,), (1,)), ((), ())), preferred_element_type=F32
-    ).astype(BF)
     grads = (g0, g1)
     for h in range(2):
-        grads[h][pl.ds(2 * col, 2)] = agg_grad[:, h * H : (h + 1) * H].reshape(2, T, H)
+        agg_grad = lax.dot_general(
+            weight[h * H : (h + 1) * H, :], pre_grad, (((1,), (1,)), ((), ())), preferred_element_type=F32
+        ).astype(BF)
+        for t in range(2):
+            grads[h][2 * col + t] = agg_grad[:, t * T : (t + 1) * T]
 
     gz = {}
     gx = {}
 
     def origin(k, d):
-        return grads_at(col_at(4 - k if k else 0, d))
-
-    def grads_at(block):
-        return pl.ds(2 * block, 2)
+        return pl.ds(2 * col_at((0, 4 - side, 2, side)[k], d), 2)
 
     def spread(h, k):
         came = grads[h].at[origin(k, 0)]
         gx[h, k, 0] = send(came, came, gx_send.at[h, k, 0], gx_recv.at[h, k, 0], ahead)
         gx[h, k, 1] = send(came, came, gx_send.at[h, k, 1], gx_recv.at[h, k, 1], behind)
+        if (h, k) in GRADS_X_STRAIGHT:
+            gx[h, k, 2] = send(came, came, gx_send.at[h, k, 2], gx_recv.at[h, k, 2], far)
 
     def pass_on(h, k):
+        if (h, k) in GRADS_X_STRAIGHT:
+            return
         gx[h, k, 0].wait_recv()
         came = grads[h].at[origin(k, 4 - side)]
         gx[h, k, 2] = send(came, came, gx_send.at[h, k, 2], gx_recv.at[h, k, 2], ahead)
 
     def spread_z(h, k):
-        mine = grads[h].at[pl.ds(2 * col, 2)]
-        gz[h, k] = send(mine, mine, gz_send.at[h, k - 1], gz_recv.at[h, k - 1], (row, col_at(k, 0)))
+        straight = h in GRADS_Z_STRAIGHT
+        block = grads[h].at[origin(1 if k == 2 and not straight else 0, 0)]
+        device = (ahead_z, far_z if straight else ahead_z, behind_z)[k - 1]
+        gz[h, k] = send(block, block, gz_send.at[h, k - 1], gz_recv.at[h, k - 1], device)
 
     def came_z(h, k):
         gz[h, k].wait_recv()
+        if k == 1 and h not in GRADS_Z_STRAIGHT:
+            spread_z(h, 2)
         spread(h, k)
 
     spread_z(0, 1)
     spread_z(0, 3)
+    if 0 in GRADS_Z_STRAIGHT:
+        spread_z(0, 2)
     spread(0, 0)
     spread(1, 0)
 
@@ -428,23 +460,24 @@
         for n in range(7):
             rcopies[h, n].wait_recv()
             total += rrecv[h][n].astype(F32)
-        feats_grad[:, h * H : (h + 1) * H] = total.reshape(2 * T, H).astype(BF)
+        for t in range(2):
+            feats_grad[t * T : (t + 1) * T, h * H : (h + 1) * H] = total[t].T.astype(BF)
 
     w_core()
     pass_on(0, 0)
     came_z(0, 1)
-    spread_z(0, 2)
+    came_z(0, 3)
     pass_on(1, 0)
-    came_z(0, 3)
-    pass_on(0, 1)
-    w_y()
-    came_z(0, 2)
     spread_z(1, 1)
     spread_z(1, 3)
+    if 1 in GRADS_Z_STRAIGHT:
+        spread_z(1, 2)
+    pass_on(0, 1)
+    came_z(0, 2)
     pass_on(0, 3)
+    w_y()
+    came_z(1, 1)
     pass_on(0, 2)
-    came_z(1, 1)
-    spread_z(1, 2)
     came_z(1, 3)
     w_x()
     for copy in xcopies.values():

time: 102 us -> 98.2 us (0.963)
  Pallas kernels: 100 us -> 96.8 us
    pallas_call x1, Pallas kernels: 98.5 us -> 95 us  [body(): pl.pallas_call(kernel, out_shape=outs, in_specs=[hbm] * 6 + [pl.BlockSpec...]
where the time goes in v3:
time: 98.2 us; the launch traced here: 98.1 us
  Pallas kernels  96.8 us (99%)
  between operations  1.29 us (1%)
    pallas_call x1, Pallas kernels, body(): pl.pallas_call(kernel, out_shape=outs, in_specs=[hbm] * 6 + [pl.BlockSpec...  95 us

profile of v3, /device:TPU:1, one launch (start us, length us, event | category | flops | bytes accessed | tf_op | source)
XLA Modules:
  0.0 98.1 jit_solution(4748513865579335437)
XLA Ops:
  1.3 95.0 %shard_map.102 = (bf16[256,256]{1,0:T(8,128)(2,1)}, f32[256,256]{1,0:T(8,128)}, f32[1,256]{1,0:T(1,128)}, bf16[256,256]{1,0:T(8,128)(2,1)}) custom-call(bf16[256,256]{1,0:T(8,128)(2,1)} %feats_hbm.1, bf16[256,256]{1,0:T(8,128)(2,1)} %weight_hbm.1, f32[1,256]{1,0:T(1,128)} %bitcast.8, bf16[256,256]{1,0:T(8,128)(2,1)} %cotangent_hbm.1, ...), custom_call_target="tpu_custom_call" | custom-call | tf_op jit(solution)/shard_map/pallas_call | solution.py:538
  96.3 1.9 %shard_map.103 = (bf16[256,256]{1,0:T(8,128)(2,1)}, f32[256,256]{1,0:T(8,128)}, f32[1,256]{1,0:T(1,128)}, bf16[256,256]{1,0:T(8,128)(2,1)}) custom-call(bf16[256,256]{1,0:T(8,128)(2,1)} %get-tuple-element.12.refs_0_, f32[256,256]{1,0:T(8,128)} %get-tuple-element.13.refs_1_, f32[1,256]{1,0:T(1,128)} %get-tuple-element.14.refs_2_, ...), custom_call_target="tpu_custom_call" | custom-call | tf_op jit(solution)/shard_map/pallas_call | solution.py:593

commit v4 on v3

--- a/solution.py
+++ b/solution.py
@@ -500,14 +500,14 @@
 
     def row_1():
         scatter_row(0, range(4))
-        v_x()
 
     def row_2():
         scatter_row(0, range(4, 8))
-        v_y()
+        v_x()
 
     tile_sums(order, tiles, g1, p1, True, (row_1, row_2))
     scatter_core(1)
+    v_y()
     scatter_row(1)
     v_core()
     finish_feats(0)

time: 98.2 us -> 95.9 us (0.977)
  Pallas kernels: 96.8 us -> 94.5 us
    pallas_call x1, Pallas kernels: 95 us -> 92.6 us  [body(): pl.pallas_call(kernel, out_shape=outs, in_specs=[hbm] * 6 + [pl.BlockSpec...]
where the time goes in v4:
time: 95.9 us; the launch traced here: 95.8 us
  Pallas kernels  94.5 us (99%)
  between operations  1.29 us (1%)
    pallas_call x1, Pallas kernels, body(): pl.pallas_call(kernel, out_shape=outs, in_specs=[hbm] * 6 + [pl.BlockSpec...  92.6 us

profile of v4, /device:TPU:1, one launch (start us, length us, event | category | flops | bytes accessed | tf_op | source)
XLA Modules:
  0.0 95.8 jit_solution(3832407756678584759)
XLA Ops:
  1.3 92.6 %shard_map.102 = (bf16[256,256]{1,0:T(8,128)(2,1)}, f32[256,256]{1,0:T(8,128)}, f32[1,256]{1,0:T(1,128)}, bf16[256,256]{1,0:T(8,128)(2,1)}) custom-call(bf16[256,256]{1,0:T(8,128)(2,1)} %feats_hbm.1, bf16[256,256]{1,0:T(8,128)(2,1)} %weight_hbm.1, f32[1,256]{1,0:T(1,128)} %bitcast.8, bf16[256,256]{1,0:T(8,128)(2,1)} %cotangent_hbm.1, ...), custom_call_target="tpu_custom_call" | custom-call | tf_op jit(solution)/shard_map/pallas_call | solution.py:538
  93.9 1.9 %shard_map.103 = (bf16[256,256]{1,0:T(8,128)(2,1)}, f32[256,256]{1,0:T(8,128)}, f32[1,256]{1,0:T(1,128)}, bf16[256,256]{1,0:T(8,128)(2,1)}) custom-call(bf16[256,256]{1,0:T(8,128)(2,1)} %get-tuple-element.12.refs_0_, f32[256,256]{1,0:T(8,128)} %get-tuple-element.13.refs_1_, f32[1,256]{1,0:T(1,128)} %get-tuple-element.14.refs_2_, ...), custom_call_target="tpu_custom_call" | custom-call | tf_op jit(solution)/shard_map/pallas_call | solution.py:593
